TPU v7x, 32 devices: a whole 2x2x4 slice. The times are simulated.
32 devices in a mesh: dp: 8 (over z, y), sub: 4 (over x, core).
Axes of the slice: x: 2, y: 2, z: 4, core: 2. Of those that a mesh axis runs over, the one named last changes fastest.
Arguments:
- activations: bfloat16 [6144, 5632], P(('dp', 'sub')), may hold values from -6 to 6
- grad_out: bfloat16 [6144, 1408], P(('dp', 'sub'))
- q_prev: bfloat16 [1408, 32], replicated, may hold values from -0.15625 to 0.15625
Outputs:
- grad_approx: float32 [5632, 1408], P('sub')
- q_new: float32 [1408, 32], replicated
All inputs are finite; a program needn't handle non-finite values.
Results may differ from a plain program's by a relative error of at most 0.0036.
Values may be sent and summed in bfloat16 or wider, within the bound.
A program may use at most 64 MiB of HBM per device.

v0:
```python
import jax
import jax.numpy as jnp
from jax import lax
from jax.sharding import PartitionSpec as P


def orthonormal(rows_part, gram):
    lower = lax.linalg.cholesky(gram)
    return lax.linalg.triangular_solve(
        lower, rows_part, left_side=False, lower=True, transpose_a=True
    )


def per_device(activations, grad_out, q_prev):
    u_low = jnp.dot(grad_out, q_prev, preferred_element_type=jnp.float32).astype(jnp.bfloat16)
    p_local = jnp.einsum("tf,tr->fr", activations, u_low, preferred_element_type=jnp.float32)
    hidden = activations.shape[1]
    block_rows = hidden // lax.axis_size("sub")
    p_sum = lax.psum(p_local, ("dp", "sub"))
    gram = jnp.dot(p_sum.T, p_sum, precision=lax.Precision.HIGHEST)
    p_hat = orthonormal(p_sum, gram)
    p_low = p_hat.astype(jnp.bfloat16)
    my_hat = lax.dynamic_slice_in_dim(p_hat, lax.axis_index("sub") * block_rows, block_rows, 0)
    v_low = jnp.dot(activations, p_low, preferred_element_type=jnp.float32).astype(jnp.bfloat16)
    q_local = jnp.einsum("tc,tr->cr", grad_out, v_low, preferred_element_type=jnp.float32)
    q_sum = lax.psum(q_local, ("dp", "sub"))
    q_new = q_sum / (lax.axis_size("dp") * lax.axis_size("sub"))
    grad_approx = jnp.dot(my_hat, q_new.T, precision=lax.Precision.HIGHEST)
    return (grad_approx, q_new)


def solution(mesh):
    in_specs = (P(("dp", "sub"), None), P(("dp", "sub"), None), P())
    out_specs = (P("sub", None), P())
    return jax.shard_map(
        per_device, mesh=mesh, in_specs=in_specs, out_specs=out_specs, check_vma=False
    )
```

profile of v0, /device:TPU:0, one launch (start us, length us, event | category | flops | bytes accessed | tf_op | source)
XLA Modules:
  0.0 296.4 jit_solution(17376727021004415565)
XLA Ops:
  7.2 0.0 copy-start
  7.2 0.0 all-reduce.3.cloned.1.call-start
  7.2 1.6 copy-done
  8.8 2.9 convolution_bitcast_fusion
  11.7 0.0 copy-start.1
  11.7 0.0 all-reduce.3.cloned.1.call-update
  11.7 0.0 all-reduce.5.cloned.1.call-start
  11.7 132.6 %all-reduce.3.cloned.1.call-done = f32[5632,32]{0,1:T(8,128)} async-done(((f32[5632,32]{0,1:T(8,128)}), f32[5632,32]{0,1:T(8,128)}) %all-reduce.3.cloned.1.call-update) | async-done | bytes 720912 | tf_op jit(solution)/shard_map/psum | solution.py:19
  144.3 2.0 fusion.9
  146.4 0.1 copy.5
  146.4 2.9 cholesky.16
  149.4 0.6 compare_reduce_fusion
  150.0 0.7 fusion.4
  150.7 2.4 custom-call.5
  153.1 1.9 fusion.5
  155.0 0.0 copy-done.1
  155.1 1.8 convolution_bitcast_fusion.1
  156.8 0.0 all-reduce.5.cloned.1.call-update
  156.8 122.7 %all-reduce.5.cloned.1.call-done = f32[1408,32]{0,1:T(8,128)} async-done(((f32[1408,32]{0,1:T(8,128)}), f32[1408,32]{0,1:T(8,128)}) %all-reduce.5.cloned.1.call-update) | async-done | bytes 180240 | tf_op jit(solution)/shard_map/psum | solution.py:26
  279.6 0.9 broadcast_multiply_fusion
  280.5 0.0 copy-start.2
  280.5 9.0 %fusion.2 = f32[1408,1408]{1,0:T(8,128)} fusion(f32[1408,32]{0,1:T(8,128)S(1)} %broadcast_multiply_fusion, f32[5632,32]{0,1:T(8,128)S(1)} %fusion.5, s32[]{:T(128)S(6)} %select_n.7), kind=kOutput, calls=%fused_computation.5 | convolution fusion | flops 761266176 | bytes 8290308 | tf_op jit(solution)/shard_map/dot_general | solution.py:28
  289.6 0.0 copy-done.2
  (2 shorter events, 0.0 us)
Async XLA Ops:
  7.2 1.6 copy-start
  7.2 137.1 %all-reduce.3.cloned.1.call-start = ((), (), s32[]{:S(2)}) async-start(), calls=%async_computation | async-start | bytes 1441792 | tf_op jit(solution)/shard_map/psum | solution.py:19
  11.7 143.4 %copy-start.1 = (bf16[192,1408]{1,0:T(8,128)(2,1)S(1)}, bf16[192,1408]{1,0:T(8,128)(2,1)}, u32[]{:S(2)}) copy-start(bf16[192,1408]{1,0:T(8,128)(2,1)} %param.4) | copy-start | bytes 1622020
  11.7 267.9 %all-reduce.5.cloned.1.call-start = ((), (), s32[]{:S(2)}) async-start(), calls=%async_computation.1 | async-start | bytes 360448 | tf_op jit(solution)/shard_map/psum | solution.py:26
  280.5 9.0 %copy-start.2 = (f32[1408,32]{0,1:T(8,128)}, f32[1408,32]{0,1:T(8,128)S(1)}, u32[]{:S(2)}) copy-start(f32[1408,32]{0,1:T(8,128)S(1)} %broadcast_multiply_fusion) | copy-start | bytes 540676
Sparse Core Ops, SparseCore 0:
  13.8 130.4 all-reduce.2
  157.0 122.5 all-reduce.4
where the time goes:
time: 298 us; the launch traced here: 296 us
  waiting for transfers between devices  255 us (86%)
  matrix products  17.6 us (6%)
  between operations  14.1 us (5%)
  other arithmetic  7.62 us (3%)
    psum x1, waiting for transfers between devices, per_device(): p_sum = lax.psum(p_local, ('dp', 'sub'))  133 us
    psum x1, waiting for transfers between devices, per_device(): q_sum = lax.psum(q_local, ('dp', 'sub'))  123 us
    dot_general x1, matrix products, per_device(): grad_approx = jnp.dot(my_hat, q_new.T, precision=lax.Precision.HIGHEST)  9.01 us
  transfers between devices with their start and end apart: 2, of which 2 were waited for; matrix products, arithmetic and copies ran while one was open for 0% of the time, Pallas kernels for 0%

commit v1 on v0

v1 whole, which is shorter than its diff:
```python
import functools

import jax
import jax.numpy as jnp
from jax import lax
from jax.experimental import pallas as pl
from jax.experimental.pallas import tpu as pltpu
from jax.sharding import PartitionSpec as P

MESH = pl.DeviceIdType.MESH
F32 = jnp.float32
BF16 = jnp.bfloat16
HIGHEST = lax.Precision.HIGHEST
LANES = 128
HALF = 16


def dot(a, b, dims=((1,), (0,)), precision=None):
    return lax.dot_general(a, b, (dims, ((), ())), precision=precision, preferred_element_type=F32)


def inverse_factor(gram):
    rank = gram.shape[0]
    row = lax.broadcasted_iota(jnp.int32, (rank, rank), 0)
    column = lax.broadcasted_iota(jnp.int32, (rank, rank), 1)
    row2 = lax.broadcasted_iota(jnp.int32, (rank, 2 * rank), 0)
    work = jnp.concatenate([gram, jnp.where(row == column, 1.0, 0.0).astype(F32)], axis=1)
    for j in range(rank):
        scale = lax.rsqrt(work[j : j + 1, j : j + 1])
        pivot = work[j : j + 1, :] * scale
        factor = work[:, j : j + 1] * scale
        work = jnp.where(row2 > j, work - factor * pivot, jnp.where(row2 == j, pivot, work))
    return work[:, rank:]


def split(x):
    high = x.astype(BF16)
    return high, (x - high.astype(F32)).astype(BF16)


def factors_kernel(
    n_dp, n_sub, a_ref, g_ref, q_ref, left_ref, q_out_ref,
    s1_send, s1_recv, part, s2_recv, whole, grams, blocks, q_local, q_recv,
    s1_s, s1_r, s2_s, s2_r, g2_s, g2_r, gm_s, gm_r, b_s, b_r, qs_s, qs_r, qg_s, qg_r,
):
    dp, sub = lax.axis_index("dp"), lax.axis_index("sub")
    n = n_dp * n_sub
    me = dp * n_sub + sub
    block = a_ref.shape[1] // n_sub
    rank = q_ref.shape[1]
    width = part.shape[1] // (n_dp // 2)
    units = 2 * (g_ref.shape[1] // LANES)

    def device(flat):
        return (flat // n_sub, flat % n_sub)

    def piece(ref, owner):
        return ref.at[pl.ds(pl.multiple_of((owner % 2) * HALF, HALF), HALF),
                      pl.ds(pl.multiple_of((owner // 2) * width, LANES), width)]

    def unit(ref, owner):
        return ref.at[pl.ds(pl.multiple_of((owner % 2) * HALF, HALF), HALF),
                      pl.ds(pl.multiple_of((owner // 2) * LANES, LANES), LANES)]

    def columns(s):
        return a_ref[:, pl.ds(pl.multiple_of(s * block, LANES), block)]

    def send(src, dst, s, r, to):
        return pltpu.make_async_remote_copy(
            src_ref=src, dst_ref=dst, send_sem=s, recv_sem=r, device_id=to, device_id_type=MESH)

    barrier = pltpu.get_barrier_semaphore()

    def greet(k, carry):
        pl.semaphore_signal(barrier, inc=1, device_id=device((me + k) % n), device_id_type=MESH)
        return carry

    lax.fori_loop(1, n, greet, 0)

    u = dot(g_ref[...], q_ref[...]).astype(BF16)
    first = []
    for k in range(1, n_sub):
        s = (sub + k) % n_sub
        s1_send[k - 1] = dot(u, columns(s), ((0,), (0,))).astype(BF16)
        if k == 1:
            pl.semaphore_wait(barrier, n - 1)
        copy = send(s1_send.at[k - 1], s1_recv.at[k - 1], s1_s.at[k - 1], s1_r.at[k - 1], (dp, s))
        copy.start()
        first.append(copy)
    total = dot(u, columns(sub), ((0,), (0,)))
    for k in range(1, n_sub):
        first[k - 1].wait_recv()
        total = total + s1_recv[k - 1].astype(F32)
    part[:, pl.ds(0, block)] = total
    if part.shape[1] > block:
        part[:, pl.ds(block, part.shape[1] - block)] = jnp.zeros((rank, part.shape[1] - block), F32)

    second = []
    for k in range(1, n_dp):
        t = (dp + k) % n_dp
        copy = send(piece(part, t), s2_recv.at[k - 1], s2_s.at[k - 1], s2_r.at[k - 1], (t, sub))
        copy.start()
        second.append(copy)
    mine = piece(part, dp)[...]
    for k in range(1, n_dp):
        second[k - 1].wait_recv()
        mine = mine + s2_recv[k - 1]
    piece(whole, dp)[...] = mine
    third = []
    for k in range(1, n_dp):
        t = (dp + k) % n_dp
        copy = send(piece(whole, dp), piece(whole, dp), g2_s.at[k - 1], g2_r.at[k - 1], (t, sub))
        copy.start()
        third.append(copy)
    for k in range(1, n_dp):
        other = (dp + n_dp - k) % n_dp
        send(piece(whole, other), piece(whole, other), g2_s.at[k - 1], g2_r.at[k - 1], (other, sub)).wait_recv()

    p = whole[:, pl.ds(0, block)]
    blocks[sub] = p.astype(BF16)
    gram = dot(p, p, ((1,), (1,)), HIGHEST)
    grams[sub] = jnp.concatenate([gram, jnp.zeros((rank, LANES - rank), F32)], axis=1)
    fourth = []
    for k in range(1, n_sub):
        s = (sub + k) % n_sub
        copy = send(grams.at[sub], grams.at[sub], gm_s.at[k - 1], gm_r.at[k - 1], (dp, s))
        copy.start()
        fourth.append(copy)
    for k in range(1, n_sub):
        s = (sub + k) % n_sub
        copy = send(blocks.at[sub], blocks.at[sub], b_s.at[k - 1], b_r.at[k - 1], (dp, s))
        copy.start()
        fourth.append(copy)
    v = dot(blocks[sub], columns(sub), ((1,), (1,)))
    for k in range(1, n_sub):
        s = (sub + n_sub - k) % n_sub
        send(grams.at[s], grams.at[s], gm_s.at[k - 1], gm_r.at[k - 1], (dp, s)).wait_recv()
    gram = grams[0]
    for s in range(1, n_sub):
        gram = gram + grams[s]
    inverse = inverse_factor(gram[:, :rank])
    high, low = split(dot(inverse, p, precision=HIGHEST))
    left_ref[pl.ds(0, rank), :] = high
    left_ref[pl.ds(rank, rank), :] = high
    left_ref[pl.ds(2 * rank, rank), :] = low

    for k in range(1, n_sub):
        s = (sub + n_sub - k) % n_sub
        send(blocks.at[s], blocks.at[s], b_s.at[k - 1], b_r.at[k - 1], (dp, s)).wait_recv()
        v = v + dot(blocks[s], columns(s), ((1,), (1,)))
    v_low = dot(inverse, v, precision=HIGHEST).astype(BF16)
    q_local[...] = dot(v_low, g_ref[...])

    def scatter(k, carry):
        t = (me + k) % n

        @pl.when(t < units)
        def _():
            send(unit(q_local, t), q_recv.at[k - 1], qs_s.at[k - 1], qs_r.at[k - 1], device(t)).start()

        return carry

    lax.fori_loop(1, n, scatter, 0)

    @pl.when(me < units)
    def _():
        def add(k, total):
            send(unit(q_local, me), q_recv.at[k - 1], qs_s.at[k - 1], qs_r.at[k - 1], device((me + k) % n)).wait_recv()
            return total + q_recv[k - 1]

        total = lax.fori_loop(1, n, add, unit(q_local, me)[...])
        unit(q_out_ref, me)[...] = total * (1.0 / n)

        def spread(k, carry):
            send(unit(q_out_ref, me), unit(q_out_ref, me), qg_s.at[k - 1], qg_r.at[me], device((me + k) % n)).start()
            return carry

        lax.fori_loop(1, n, spread, 0)

    def collect(k, carry):
        t = (me + n - k) % n

        @pl.when(t < units)
        def _():
            send(unit(q_out_ref, t), unit(q_out_ref, t), qg_s.at[k - 1], qg_r.at[t], device(t)).wait_recv()

        return carry

    lax.fori_loop(1, n, collect, 0)

    for copy in first + second + third + fourth:
        copy.wait_send()

    def drain(k, carry):
        t = (me + k) % n

        @pl.when(t < units)
        def _():
            send(unit(q_local, t), q_recv.at[k - 1], qs_s.at[k - 1], qs_r.at[k - 1], device(t)).wait_send()

        @pl.when(me < units)
        def _():
            send(unit(q_out_ref, me), unit(q_out_ref, me), qg_s.at[k - 1], qg_r.at[me], device(t)).wait_send()

        return carry

    lax.fori_loop(1, n, drain, 0)


def result_kernel(left_ref, q_ref, grad_ref, q_new_ref, right):
    rank = q_ref.shape[0]

    @pl.when(pl.program_id(0) == 0)
    def _():
        high, low = split(q_ref[...])
        right[pl.ds(0, rank), :] = high
        right[pl.ds(rank, rank), :] = low
        right[pl.ds(2 * rank, rank), :] = high
        q_new_ref[...] = q_ref[...].T

    grad_ref[...] = dot(left_ref[...], right[...], ((0,), (0,)))


def fast(n_dp, n_sub, activations, grad_out, q_prev):
    hidden, channels, rank = activations.shape[1], grad_out.shape[1], q_prev.shape[1]
    block = hidden // n_sub
    groups = n_dp // 2
    width = -(-(block // LANES) // groups) * LANES
    n = n_dp * n_sub
    dma = pltpu.SemaphoreType.DMA
    vmem = pl.BlockSpec(memory_space=pltpu.VMEM)
    left, q_t = pl.pallas_call(
        functools.partial(factors_kernel, n_dp, n_sub),
        out_shape=(
            jax.ShapeDtypeStruct((3 * rank, block), BF16),
            jax.ShapeDtypeStruct((rank, channels), F32),
        ),
        in_specs=[vmem] * 3,
        out_specs=(vmem, vmem),
        scratch_shapes=[
            pltpu.VMEM((n_sub - 1, rank, block), BF16),
            pltpu.VMEM((n_sub - 1, rank, block), BF16),
            pltpu.VMEM((rank, groups * width), F32),
            pltpu.VMEM((n_dp - 1, HALF, width), F32),
            pltpu.VMEM((rank, groups * width), F32),
            pltpu.VMEM((n_sub, rank, LANES), F32),
            pltpu.VMEM((n_sub, rank, block), BF16),
            pltpu.VMEM((rank, channels), F32),
            pltpu.VMEM((n - 1, HALF, LANES), F32),
            dma((n_sub - 1,)), dma((n_sub - 1,)),
            dma((n_dp - 1,)), dma((n_dp - 1,)),
            dma((n_dp - 1,)), dma((n_dp - 1,)),
            dma((n_sub - 1,)), dma((n_sub - 1,)),
            dma((n_sub - 1,)), dma((n_sub - 1,)),
            dma((n - 1,)), dma((n - 1,)),
            dma((n - 1,)), dma((n,)),
        ],
        compiler_params=pltpu.CompilerParams(
            collective_id=0, has_side_effects=True, vmem_limit_bytes=32 * 2**20
        ),
        name="factors",
    )(activations, grad_out, q_prev)
    return pl.pallas_call(
        result_kernel,
        grid=(block // LANES,),
        out_shape=(
            jax.ShapeDtypeStruct((block, channels), F32),
            jax.ShapeDtypeStruct((channels, rank), F32),
        ),
        in_specs=[
            pl.BlockSpec((3 * rank, LANES), lambda i: (0, i)),
            pl.BlockSpec((rank, channels), lambda i: (0, 0)),
        ],
        out_specs=(
            pl.BlockSpec((LANES, channels), lambda i: (i, 0)),
            pl.BlockSpec((channels, rank), lambda i: (0, 0)),
        ),
        scratch_shapes=[pltpu.VMEM((3 * rank, channels), BF16)],
        compiler_params=pltpu.CompilerParams(vmem_limit_bytes=32 * 2**20),
        name="result",
    )(left, q_t)


def general(activations, grad_out, q_prev):
    u_low = jnp.dot(grad_out, q_prev, preferred_element_type=F32).astype(BF16)
    p_local = jnp.einsum("tf,tr->fr", activations, u_low, preferred_element_type=F32)
    block_rows = activations.shape[1] // lax.axis_size("sub")
    p_sum = lax.psum(p_local, ("dp", "sub"))
    gram = jnp.dot(p_sum.T, p_sum, precision=HIGHEST)
    lower = lax.linalg.cholesky(gram)
    p_hat = lax.linalg.triangular_solve(lower, p_sum, left_side=False, lower=True, transpose_a=True)
    p_low = p_hat.astype(BF16)
    my_hat = lax.dynamic_slice_in_dim(p_hat, lax.axis_index("sub") * block_rows, block_rows, 0)
    v_low = jnp.dot(activations, p_low, preferred_element_type=F32).astype(BF16)
    q_local = jnp.einsum("tc,tr->cr", grad_out, v_low, preferred_element_type=F32)
    q_sum = lax.psum(q_local, ("dp", "sub"))
    q_new = q_sum / (lax.axis_size("dp") * lax.axis_size("sub"))
    grad_approx = jnp.dot(my_hat, q_new.T, precision=HIGHEST)
    return (grad_approx, q_new)


def solution(mesh):
    n_dp, n_sub = mesh.shape["dp"], mesh.shape["sub"]

    def per_device(activations, grad_out, q_prev):
        hidden, channels, rank = activations.shape[1], grad_out.shape[1], q_prev.shape[1]
        fits = (
            n_dp % 2 == 0
            and n_sub > 1
            and rank == 2 * HALF
            and hidden % (n_sub * LANES) == 0
            and channels % LANES == 0
            and 2 * channels // LANES <= n_dp * n_sub
        )
        if fits:
            return fast(n_dp, n_sub, activations, grad_out, q_prev)
        return general(activations, grad_out, q_prev)

    return jax.shard_map(
        per_device,
        mesh=mesh,
        in_specs=(P(("dp", "sub"), None), P(("dp", "sub"), None), P()),
        out_specs=(P("sub", None), P()),
        check_vma=False,
    )
```

time: 298 us -> 61.5 us (0.21)
  the two profiles are of different devices: /device:TPU:0 before, /device:TPU:25 now
where the time goes in v1:
time: 61.5 us; the launch traced here: 61.2 us
  Pallas kernels  55.9 us (91%)
  local copies, waits for them, and re-layouts  4.67 us (8%)
  between operations  0.65 us (1%)
    pallas_call x1, Pallas kernels, fast(): pl.pallas_call(functools.partial(factors_kernel, n_dp, n_sub), out_shape=...  48.7 us
    pallas_call x1, Pallas kernels, fast(): pl.pallas_call(result_kernel, grid=(block // LANES,), out_shape=(jax.Shap...  7.2 us
    unnamed x5, local copies, waits for them, and re-layouts  3.76 us

profile of v1, /device:TPU:25, one launch (start us, length us, event | category | flops | bytes accessed | tf_op | source)
XLA Modules:
  0.0 61.2 jit_solution(14279610135500851159)
XLA Ops:
  0.6 1.1 %copy.5.q_ref = bf16[1408,32]{1,0:T(8,128)(2,1)S(1)} copy(bf16[1408,32]{0,1:T(8,128)(2,1)} %param.5) | data formatting | bytes 180224 | tf_op args[2]
  1.7 0.0 copy-start
  1.8 1.6 %copy-done = bf16[192,5632]{1,0:T(8,128)(2,1)S(1)} copy-done((bf16[192,5632]{1,0:T(8,128)(2,1)S(1)}, bf16[192,5632]{1,0:T(8,128)(2,1)}, u32[]{:S(2)}) %copy-start) | copy-done | bytes 2162712
  3.4 0.0 copy-start.1
  3.4 1.0 %copy-done.1 = bf16[192,1408]{1,0:T(8,128)(2,1)S(1)} copy-done((bf16[192,1408]{1,0:T(8,128)(2,1)S(1)}, bf16[192,1408]{1,0:T(8,128)(2,1)}, u32[]{:S(2)}) %copy-start.1) | copy-done | bytes 540696
  4.4 48.7 %factors.1 = (bf16[96,1408]{1,0:T(8,128)(2,1)S(1)}, f32[32,1408]{1,0:T(8,128)S(1)}) custom-call(bf16[192,5632]{1,0:T(8,128)(2,1)S(1)} %copy-done, bf16[192,1408]{1,0:T(8,128)(2,1)S(1)} %copy-done.1, bf16[1408,32]{1,0:T(8,128)(2,1)S(1)} %copy.5.q_ref), custom_call_target="tpu_custom_call" | custom-call | tf_op jit(solution)/shard_map/factors/pallas_call | solution.py:232
  53.1 7.2 %result.1 = (f32[1408,1408]{1,0:T(8,128)}, f32[1408,32]{1,0:T(8,128)S(1)}) custom-call(bf16[96,1408]{1,0:T(8,128)(2,1)S(1)} %get-tuple-element.4.left_ref, f32[32,1408]{1,0:T(8,128)S(1)} %get-tuple-element.5.q_ref), custom_call_target="tpu_custom_call" | custom-call | tf_op jit(solution)/shard_map/result/pallas_call | solution.py:263
  60.3 0.9 %copy.6 = f32[1408,32]{0,1:T(8,128)} copy(f32[1408,32]{1,0:T(8,128)S(1)} %get-tuple-element.7) | data formatting | bytes 360448 | tf_op jit(solution)/shard_map/result/pallas_call | solution.py:263
Async XLA Ops:
  1.7 1.6 %copy-start = (bf16[192,5632]{1,0:T(8,128)(2,1)S(1)}, bf16[192,5632]{1,0:T(8,128)(2,1)}, u32[]{:S(2)}) copy-start(bf16[192,5632]{1,0:T(8,128)(2,1)} %a_ref.1) | copy-start | bytes 6488068
  3.4 1.0 %copy-start.1 = (bf16[192,1408]{1,0:T(8,128)(2,1)S(1)}, bf16[192,1408]{1,0:T(8,128)(2,1)}, u32[]{:S(2)}) copy-start(bf16[192,1408]{1,0:T(8,128)(2,1)} %g_ref.1) | copy-start | bytes 1622020

commit v2 on v0

v2 whole, which is shorter than its diff:
```python
import functools

import jax
import jax.numpy as jnp
from jax import lax
from jax.experimental import pallas as pl
from jax.experimental.pallas import tpu as pltpu
from jax.sharding import PartitionSpec as P

MESH = pl.DeviceIdType.MESH
F32 = jnp.float32
BF16 = jnp.bfloat16
HIGHEST = lax.Precision.HIGHEST
LANES = 128
HALF = 16
ROWS = 256
HBM = pltpu.MemorySpace.HBM


def dot(a, b, dims=((1,), (0,)), precision=None):
    return lax.dot_general(a, b, (dims, ((), ())), precision=precision, preferred_element_type=F32)


def inverse_factor(gram):
    rank = gram.shape[0]
    row = lax.broadcasted_iota(jnp.int32, (rank, rank), 0)
    column = lax.broadcasted_iota(jnp.int32, (rank, rank), 1)
    row2 = lax.broadcasted_iota(jnp.int32, (rank, 2 * rank), 0)
    work = jnp.concatenate([gram, jnp.where(row == column, 1.0, 0.0).astype(F32)], axis=1)
    for j in range(rank):
        scale = lax.rsqrt(work[j : j + 1, j : j + 1])
        pivot = work[j : j + 1, :] * scale
        factor = work[:, j : j + 1] * scale
        work = jnp.where(row2 > j, work - factor * pivot, jnp.where(row2 == j, pivot, work))
    return work[:, rank:]


def split(x):
    high = x.astype(BF16)
    return high, (x - high.astype(F32)).astype(BF16)


def dot_split(a, b):
    a_high, a_low = split(a)
    b_high, b_low = split(b)
    return dot(jnp.concatenate([a_high, a_high, a_low], 1), jnp.concatenate([b_high, b_low, b_high], 0))


def factors_kernel(
    n_dp, n_sub, a_hbm, g_hbm, q_hbm, left_ref, q_all,
    a_ref, g_ref, q_ref, s1_send, s1_recv, part, part_low, s2_recv, whole_high, whole_low, grams, blocks,
    q_local, q_send, qa_recv, q_parts,
    in_s, a_s, s1_s, s1_r, s2_s, s2_r, gh_s, gh_r, gl_s, gl_r, gm_s, gm_r, b_s, b_r,
    qa_s, qa_r, qb_s, qb_r, qc_s, qc_r,
):
    dp, sub = lax.axis_index("dp"), lax.axis_index("sub")
    n = n_dp * n_sub
    block = a_ref.shape[1] // n_sub
    rank, channels = q_ref.shape
    width = part.shape[1] // (n_dp // 2)
    q_width = q_all.shape[1] // (n_dp // 2)
    dp_to = [None] + [(dp + k) % n_dp for k in range(1, n_dp)]
    dp_from = [None] + [(dp + n_dp - k) % n_dp for k in range(1, n_dp)]
    sub_to = [sub] + [(sub + k) % n_sub for k in range(1, n_sub)]
    sub_from = [sub] + [(sub + n_sub - k) % n_sub for k in range(1, n_sub)]

    def piece(ref, owner, wide):
        return ref.at[pl.ds(pl.multiple_of((owner % 2) * HALF, HALF), HALF),
                      pl.ds(pl.multiple_of((owner // 2) * wide, LANES), wide)]

    def columns(ref, s, wide):
        return ref.at[:, pl.ds(pl.multiple_of(s * wide, LANES), wide)]

    def send(src, dst, s, r, to):
        return pltpu.make_async_remote_copy(
            src_ref=src, dst_ref=dst, send_sem=s, recv_sem=r, device_id=to, device_id_type=MESH)

    sent = []

    def start(*copy):
        copy = send(*copy)
        copy.start()
        sent.append(copy)

    barrier = pltpu.get_barrier_semaphore()
    for k in range(1, n_sub):
        pl.semaphore_signal(barrier, inc=1, device_id=(dp, sub_to[k]), device_id_type=MESH)
    for k in range(1, n_dp):
        pl.semaphore_signal(barrier, inc=1, device_id=(dp_to[k], sub), device_id_type=MESH)

    load_g = pltpu.make_async_copy(g_hbm, g_ref, in_s.at[0])
    load_q = pltpu.make_async_copy(q_hbm, q_ref, in_s.at[1])
    load_g.start()
    load_q.start()
    loads = []
    for k in list(range(1, n_sub)) + [0]:
        load = pltpu.make_async_copy(columns(a_hbm, sub_to[k], block), columns(a_ref, sub_to[k], block), a_s.at[k])
        load.start()
        loads.append(load)
    load_g.wait()
    load_q.wait()
    u = dot(q_ref[...], g_ref[...], ((1,), (1,))).astype(BF16)
    for k in range(1, n_sub):
        loads[k - 1].wait()
        s1_send[k - 1] = dot(u, columns(a_ref, sub_to[k], block)[...]).astype(BF16)
        if k == 1:
            pl.semaphore_wait(barrier, n_sub + n_dp - 2)
        start(s1_send.at[k - 1], s1_recv.at[k - 1], s1_s.at[k - 1], s1_r.at[k - 1], (dp, sub_to[k]))
    loads[n_sub - 1].wait()
    total = dot(u, columns(a_ref, sub, block)[...])
    for k in range(1, n_sub):
        send(s1_send.at[k - 1], s1_recv.at[k - 1], s1_s.at[k - 1], s1_r.at[k - 1], (dp, sub_to[k])).wait_recv()
        total = total + s1_recv[k - 1].astype(F32)
    part[:, pl.ds(0, block)] = total
    part_low[:, pl.ds(0, block)] = total.astype(BF16)
    if part.shape[1] > block:
        rest = part.shape[1] - block
        part[:, pl.ds(block, rest)] = jnp.zeros((rank, rest), F32)
        part_low[:, pl.ds(block, rest)] = jnp.zeros((rank, rest), BF16)

    for k in range(1, n_dp):
        start(piece(part_low, dp_to[k], width), s2_recv.at[k - 1], s2_s.at[k - 1], s2_r.at[k - 1], (dp_to[k], sub))
    mine = piece(part, dp, width)[...]
    for k in range(1, n_dp):
        send(piece(part_low, dp_to[k], width), s2_recv.at[k - 1], s2_s.at[k - 1], s2_r.at[k - 1], (dp_to[k], sub)).wait_recv()
        mine = mine + s2_recv[k - 1].astype(F32)
    high, low = split(mine)
    high_piece, low_piece = piece(whole_high, dp, width), piece(whole_low, dp, width)
    high_piece[...] = high
    low_piece[...] = low
    for k in range(1, n_dp):
        start(high_piece, high_piece, gh_s.at[k - 1], gh_r.at[k - 1], (dp_to[k], sub))
    for k in range(1, n_dp):
        other = piece(whole_high, dp_from[k], width)
        send(other, other, gh_s.at[k - 1], gh_r.at[k - 1], (dp_from[k], sub)).wait_recv()

    p_high = whole_high[:, pl.ds(0, block)]
    gram = dot(p_high, p_high, ((1,), (1,)))
    grams[sub] = jnp.concatenate([gram, jnp.zeros((rank, LANES - rank), F32)], axis=1)
    for k in range(1, n_sub):
        start(grams.at[sub], grams.at[sub], gm_s.at[k - 1], gm_r.at[k - 1], (dp, sub_to[k]))
    for k in range(1, n_sub):
        start(whole_high.at[:, pl.ds(0, block)], blocks.at[sub], b_s.at[k - 1], b_r.at[k - 1], (dp, sub_to[k]))
    for k in range(1, n_dp):
        start(low_piece, low_piece, gl_s.at[k - 1], gl_r.at[k - 1], (dp_to[k], sub))
    v = dot(p_high, columns(a_ref, sub, block)[...], ((1,), (1,)))
    for k in range(1, n_sub):
        other = grams.at[sub_from[k]]
        send(other, other, gm_s.at[k - 1], gm_r.at[k - 1], (dp, sub_from[k])).wait_recv()
    gram = grams[0]
    for s in range(1, n_sub):
        gram = gram + grams[s]
    inverse = inverse_factor(gram[:, :rank])

    for k in range(1, n_sub):
        other = blocks.at[sub_from[k]]
        send(other, other, b_s.at[k - 1], b_r.at[k - 1], (dp, sub_from[k])).wait_recv()
        v = v + dot(other[...], columns(a_ref, sub_from[k], block)[...], ((1,), (1,)))
    v_low = dot_split(inverse, v).astype(BF16)
    q = dot(v_low, g_ref[...])
    rest = q_all.shape[1] - channels
    if rest:
        q = jnp.concatenate([q, jnp.zeros((rank, rest), F32)], axis=1)
    q_local[...] = q
    q_send[...] = q.astype(BF16)
    for k in range(1, n_dp):
        start(piece(q_send, dp_to[k], q_width), qa_recv.at[k - 1], qa_s.at[k - 1], qa_r.at[k - 1], (dp_to[k], sub))

    for k in range(1, n_dp):
        other = piece(whole_low, dp_from[k], width)
        send(other, other, gl_s.at[k - 1], gl_r.at[k - 1], (dp_from[k], sub)).wait_recv()
    p = p_high.astype(F32) + whole_low[:, pl.ds(0, block)].astype(F32)
    high, low = split(dot_split(inverse, p))
    left_ref[pl.ds(0, rank), :] = high
    left_ref[pl.ds(rank, rank), :] = high
    left_ref[pl.ds(2 * rank, rank), :] = low

    total = piece(q_local, dp, q_width)[...]
    for k in range(1, n_dp):
        send(piece(q_send, dp_to[k], q_width), qa_recv.at[k - 1], qa_s.at[k - 1], qa_r.at[k - 1], (dp_to[k], sub)).wait_recv()
        total = total + qa_recv[k - 1].astype(F32)
    q_parts[sub] = total
    for k in range(1, n_sub):
        start(q_parts.at[sub], q_parts.at[sub], qb_s.at[k - 1], qb_r.at[k - 1], (dp, sub_to[k]))
    for k in range(1, n_sub):
        other = q_parts.at[sub_from[k]]
        send(other, other, qb_s.at[k - 1], qb_r.at[k - 1], (dp, sub_from[k])).wait_recv()
    total = q_parts[0]
    for s in range(1, n_sub):
        total = total + q_parts[s]
    mine = piece(q_all, dp, q_width)
    mine[...] = total * (1.0 / n)
    for k in range(1, n_dp):
        start(mine, mine, qc_s.at[k - 1], qc_r.at[k - 1], (dp_to[k], sub))
    for k in range(1, n_dp):
        other = piece(q_all, dp_from[k], q_width)
        send(other, other, qc_s.at[k - 1], qc_r.at[k - 1], (dp_from[k], sub)).wait_recv()

    for copy in sent:
        copy.wait_send()


def result_kernel(left_hbm, q_hbm, grad_ref, q_new_ref, left_ref, q_ref, right, held, in_s, q_s, out_s):
    rank, channels = q_new_ref.shape
    load_q = pltpu.make_async_copy(q_hbm, q_ref, in_s.at[0])
    load_left = pltpu.make_async_copy(left_hbm, left_ref, in_s.at[1])
    load_q.start()
    load_left.start()
    load_q.wait()
    copies = [pltpu.make_async_copy(q_ref.at[:, pl.ds(0, channels)], q_new_ref, q_s)]
    copies[0].start()
    high, low = split(q_ref[:, pl.ds(0, channels)])
    right[pl.ds(0, rank), :] = high
    right[pl.ds(rank, rank), :] = low
    right[pl.ds(2 * rank, rank), :] = high
    load_left.wait()
    rows = grad_ref.shape[0]
    for i, at in enumerate(range(0, rows, ROWS)):
        here = pl.ds(at, min(ROWS, rows - at))
        held[here, :] = dot(left_ref[:, here], right[...], ((0,), (0,)))
        copies.append(pltpu.make_async_copy(held.at[here], grad_ref.at[here], out_s.at[i]))
        copies[-1].start()
    for copy in copies:
        copy.wait()


def widths(n_dp, n_sub, hidden, channels):
    def share(size, parts):
        return -(-(size // LANES) // parts) * LANES

    return share(hidden // n_sub, n_dp // 2), share(channels, n_dp // 2)


def fast(n_dp, n_sub, activations, grad_out, q_prev):
    tokens, hidden = activations.shape
    channels, rank = q_prev.shape
    block = hidden // n_sub
    width, q_width = widths(n_dp, n_sub, hidden, channels)
    padded = n_dp // 2 * width
    q_padded = n_dp // 2 * q_width
    dma = pltpu.SemaphoreType.DMA
    vmem = pl.BlockSpec(memory_space=pltpu.VMEM)
    hbm = pl.BlockSpec(memory_space=HBM)
    left, q_t = pl.pallas_call(
        functools.partial(factors_kernel, n_dp, n_sub),
        out_shape=(
            jax.ShapeDtypeStruct((3 * rank, block), BF16),
            jax.ShapeDtypeStruct((rank, q_padded), F32),
        ),
        in_specs=[hbm] * 3,
        out_specs=(vmem, vmem),
        scratch_shapes=[
            pltpu.VMEM((tokens, hidden), BF16),
            pltpu.VMEM((tokens, channels), BF16),
            pltpu.VMEM((rank, channels), BF16),
            pltpu.VMEM((n_sub - 1, rank, block), BF16),
            pltpu.VMEM((n_sub - 1, rank, block), BF16),
            pltpu.VMEM((rank, padded), F32),
            pltpu.VMEM((rank, padded), BF16),
            pltpu.VMEM((n_dp - 1, HALF, width), BF16),
            pltpu.VMEM((rank, padded), BF16),
            pltpu.VMEM((rank, padded), BF16),
            pltpu.VMEM((n_sub, rank, LANES), F32),
            pltpu.VMEM((n_sub, rank, block), BF16),
            pltpu.VMEM((rank, q_padded), F32),
            pltpu.VMEM((rank, q_padded), BF16),
            pltpu.VMEM((n_dp - 1, HALF, q_width), BF16),
            pltpu.VMEM((n_sub, HALF, q_width), F32),
            dma((2,)), dma((n_sub,)),
            dma((n_sub - 1,)), dma((n_sub - 1,)),
            dma((n_dp - 1,)), dma((n_dp - 1,)),
            dma((n_dp - 1,)), dma((n_dp - 1,)),
            dma((n_dp - 1,)), dma((n_dp - 1,)),
            dma((n_sub - 1,)), dma((n_sub - 1,)),
            dma((n_sub - 1,)), dma((n_sub - 1,)),
            dma((n_dp - 1,)), dma((n_dp - 1,)),
            dma((n_sub - 1,)), dma((n_sub - 1,)),
            dma((n_dp - 1,)), dma((n_dp - 1,)),
        ],
        compiler_params=pltpu.CompilerParams(
            collective_id=0, has_side_effects=True, vmem_limit_bytes=62 * 2**20
        ),
        name="factors",
    )(activations, grad_out, q_prev.T)
    grad, q_new = pl.pallas_call(
        result_kernel,
        out_shape=(
            jax.ShapeDtypeStruct((block, channels), F32),
            jax.ShapeDtypeStruct((rank, channels), F32),
        ),
        in_specs=[hbm, hbm],
        out_specs=(hbm, hbm),
        scratch_shapes=[
            pltpu.VMEM((3 * rank, block), BF16),
            pltpu.VMEM((rank, q_padded), F32),
            pltpu.VMEM((3 * rank, channels), BF16),
            pltpu.VMEM((block, channels), F32),
            dma((2,)),
            dma,
            dma((-(-block // ROWS),)),
        ],
        compiler_params=pltpu.CompilerParams(vmem_limit_bytes=62 * 2**20),
        name="result",
    )(left, q_t)
    return grad, q_new.T


def general(activations, grad_out, q_prev):
    u_low = jnp.dot(grad_out, q_prev, preferred_element_type=F32).astype(BF16)
    p_local = jnp.einsum("tf,tr->fr", activations, u_low, preferred_element_type=F32)
    block_rows = activations.shape[1] // lax.axis_size("sub")
    p_sum = lax.psum(p_local, ("dp", "sub"))
    gram = jnp.dot(p_sum.T, p_sum, precision=HIGHEST)
    lower = lax.linalg.cholesky(gram)
    p_hat = lax.linalg.triangular_solve(lower, p_sum, left_side=False, lower=True, transpose_a=True)
    p_low = p_hat.astype(BF16)
    my_hat = lax.dynamic_slice_in_dim(p_hat, lax.axis_index("sub") * block_rows, block_rows, 0)
    v_low = jnp.dot(activations, p_low, preferred_element_type=F32).astype(BF16)
    q_local = jnp.einsum("tc,tr->cr", grad_out, v_low, preferred_element_type=F32)
    q_sum = lax.psum(q_local, ("dp", "sub"))
    q_new = q_sum / (lax.axis_size("dp") * lax.axis_size("sub"))
    grad_approx = jnp.dot(my_hat, q_new.T, precision=HIGHEST)
    return (grad_approx, q_new)


def solution(mesh):
    n_dp, n_sub = mesh.shape["dp"], mesh.shape["sub"]

    def per_device(activations, grad_out, q_prev):
        hidden, channels, rank = activations.shape[1], grad_out.shape[1], q_prev.shape[1]
        fits = (
            n_dp % 2 == 0
            and n_sub > 1
            and rank == 2 * HALF
            and hidden % (n_sub * LANES) == 0
            and channels % LANES == 0
        )
        if fits:
            return fast(n_dp, n_sub, activations, grad_out, q_prev)
        return general(activations, grad_out, q_prev)

    return jax.shard_map(
        per_device,
        mesh=mesh,
        in_specs=(P(("dp", "sub"), None), P(("dp", "sub"), None), P()),
        out_specs=(P("sub", None), P()),
        check_vma=False,
    )
```

time: 298 us -> 47.7 us (0.16)
  waiting for transfers between devices: 255 us -> 0 us
  Pallas kernels: 0 us -> 46.9 us
  matrix products: 17.6 us -> 0 us
  between operations: 14.1 us -> 0.64 us
  other arithmetic: 7.62 us -> 0 us
    psum x2 -> x0, waiting for transfers between devices: 255 us -> none  [the longest x1 133 us: per_device(): p_sum = lax.psum(p_local, ('dp', 'sub'))]
    pallas_call x0 -> x2, Pallas kernels: none -> 46.9 us  [the longest x1 42.2 us: fast(): pl.pallas_call(functools.partial(factors_kernel, n_dp, n_sub), out_shape=...]
    dot_general x4 -> x0, matrix products: 15.7 us -> none  [the longest x1 9.01 us: per_device(): grad_approx = jnp.dot(my_hat, q_new.T, precision=lax.Precision.HIGHEST)]
    another operation x5 -> x0, other arithmetic: 6.68 us -> none  [the longest x3 3.6 us: orthonormal(): lower = lax.linalg.cholesky(gram)]
  transfers between devices with their start and end apart: 2 -> 0, of which waited for: 2 -> 0; matrix products, arithmetic and copies ran while one was open for 0% -> 0% of each run, Pallas kernels for 0% -> 0%
where the time goes in v2:
time: 47.7 us; the launch traced here: 47.5 us
  Pallas kernels  46.9 us (98%)
  between operations  0.64 us (1%)
    pallas_call x1, Pallas kernels, fast(): pl.pallas_call(functools.partial(factors_kernel, n_dp, n_sub), out_shape=...  42.2 us
    pallas_call x1, Pallas kernels, fast(): pl.pallas_call(result_kernel, out_shape=(jax.ShapeDtypeStruct((block, cha...  4.67 us

profile of v2, /device:TPU:0, one launch (start us, length us, event | category | flops | bytes accessed | tf_op | source)
XLA Modules:
  0.0 47.5 jit_solution(15649720882665939030)
XLA Ops:
  0.6 42.2 %factors.1 = (bf16[96,1408]{1,0:T(8,128)(2,1)}, f32[32,1536]{1,0:T(8,128)}) custom-call(bf16[192,5632]{1,0:T(8,128)(2,1)} %a_hbm.1, bf16[192,1408]{1,0:T(8,128)(2,1)} %g_hbm.1, bf16[32,1408]{1,0:T(8,128)(2,1)} %bitcast.2), custom_call_target="tpu_custom_call" | custom-call | tf_op jit(solution)/shard_map/factors/pallas_call | solution.py:244
  42.9 4.7 %result.1 = (f32[1408,1408]{1,0:T(8,128)}, f32[32,1408]{1,0:T(8,128)}) custom-call(bf16[96,1408]{1,0:T(8,128)(2,1)} %get-tuple-element.6.left_hbm, f32[32,1536]{1,0:T(8,128)} %get-tuple-element.7.q_hbm), custom_call_target="tpu_custom_call" | custom-call | tf_op jit(solution)/shard_map/result/pallas_call | solution.py:285

commit v3 on v2

--- a/solution.py
+++ b/solution.py
@@ -61,8 +61,10 @@
     q_width = q_all.shape[1] // (n_dp // 2)
     dp_to = [None] + [(dp + k) % n_dp for k in range(1, n_dp)]
     dp_from = [None] + [(dp + n_dp - k) % n_dp for k in range(1, n_dp)]
-    sub_to = [sub] + [(sub + k) % n_sub for k in range(1, n_sub)]
-    sub_from = [sub] + [(sub + n_sub - k) % n_sub for k in range(1, n_sub)]
+    chips, chip, core = n_sub // 2, sub // 2, sub % 2
+    steps = [(x, c) for x in range(1, chips) for c in range(2)] + [(0, 1)]
+    sub_to = [sub] + [(chip + x) % chips * 2 + (core + c) % 2 for x, c in steps]
+    sub_from = [sub] + [(chip + chips - x) % chips * 2 + (core + c) % 2 for x, c in steps]
 
     def piece(ref, owner, wide):
         return ref.at[pl.ds(pl.multiple_of((owner % 2) * HALF, HALF), HALF),
@@ -152,7 +154,7 @@
         gram = gram + grams[s]
     inverse = inverse_factor(gram[:, :rank])
 
-    for k in range(1, n_sub):
+    for k in range(n_sub - 1, 0, -1):
         other = blocks.at[sub_from[k]]
         send(other, other, b_s.at[k - 1], b_r.at[k - 1], (dp, sub_from[k])).wait_recv()
         v = v + dot(other[...], columns(a_ref, sub_from[k], block)[...], ((1,), (1,)))
@@ -215,8 +217,9 @@
     right[pl.ds(2 * rank, rank), :] = high
     load_left.wait()
     rows = grad_ref.shape[0]
-    for i, at in enumerate(range(0, rows, ROWS)):
-        here = pl.ds(at, min(ROWS, rows - at))
+    edges = [0] + list(range(LANES, rows, ROWS)) + [rows]
+    for i, (at, end) in enumerate(zip(edges, edges[1:])):
+        here = pl.ds(at, end - at)
         held[here, :] = dot(left_ref[:, here], right[...], ((0,), (0,)))
         copies.append(pltpu.make_async_copy(held.at[here], grad_ref.at[here], out_s.at[i]))
         copies[-1].start()
@@ -297,7 +300,7 @@
             pltpu.VMEM((block, channels), F32),
             dma((2,)),
             dma,
-            dma((-(-block // ROWS),)),
+            dma((1 + -(-block // ROWS),)),
         ],
         compiler_params=pltpu.CompilerParams(vmem_limit_bytes=62 * 2**20),
         name="result",
@@ -330,7 +333,7 @@
         hidden, channels, rank = activations.shape[1], grad_out.shape[1], q_prev.shape[1]
         fits = (
             n_dp % 2 == 0
-            and n_sub > 1
+            and n_sub % 2 == 0
             and rank == 2 * HALF
             and hidden % (n_sub * LANES) == 0
             and channels % LANES == 0

time: 47.7 us -> 47.9 us (level)
  no operation moved by 1% of the time
where the time goes in v3:
time: 47.9 us; the launch traced here: 47.7 us
  Pallas kernels  47 us (98%)
  between operations  0.64 us (1%)
    pallas_call x1, Pallas kernels, fast(): pl.pallas_call(functools.partial(factors_kernel, n_dp, n_sub), out_shape=...  42.4 us
    pallas_call x1, Pallas kernels, fast(): pl.pallas_call(result_kernel, out_shape=(jax.ShapeDtypeStruct((block, cha...  4.63 us

profile of v3, /device:TPU:0, one launch (start us, length us, event | category | flops | bytes accessed | tf_op | source)
XLA Modules:
  0.0 47.7 jit_solution(10649837614959715666)
XLA Ops:
  0.6 42.4 %factors.1 = (bf16[96,1408]{1,0:T(8,128)(2,1)}, f32[32,1536]{1,0:T(8,128)}) custom-call(bf16[192,5632]{1,0:T(8,128)(2,1)} %a_hbm.1, bf16[192,1408]{1,0:T(8,128)(2,1)} %g_hbm.1, bf16[32,1408]{1,0:T(8,128)(2,1)} %bitcast.2), custom_call_target="tpu_custom_call" | custom-call | tf_op jit(solution)/shard_map/factors/pallas_call | solution.py:247
  43.1 4.6 %result.1 = (f32[1408,1408]{1,0:T(8,128)}, f32[32,1408]{1,0:T(8,128)}) custom-call(bf16[96,1408]{1,0:T(8,128)(2,1)} %get-tuple-element.6.left_hbm, f32[32,1536]{1,0:T(8,128)} %get-tuple-element.7.q_hbm), custom_call_target="tpu_custom_call" | custom-call | tf_op jit(solution)/shard_map/result/pallas_call | solution.py:288

commit v4 on v3

--- a/solution.py
+++ b/solution.py
@@ -59,8 +59,9 @@
     rank, channels = q_ref.shape
     width = part.shape[1] // (n_dp // 2)
     q_width = q_all.shape[1] // (n_dp // 2)
-    dp_to = [None] + [(dp + k) % n_dp for k in range(1, n_dp)]
-    dp_from = [None] + [(dp + n_dp - k) % n_dp for k in range(1, n_dp)]
+    far_first = sorted(range(1, n_dp), key=lambda k: -min(k, n_dp - k))
+    dp_to = [None] + [(dp + k) % n_dp for k in far_first]
+    dp_from = [None] + [(dp + n_dp - k) % n_dp for k in far_first]
     chips, chip, core = n_sub // 2, sub // 2, sub % 2
     steps = [(x, c) for x in range(1, chips) for c in range(2)] + [(0, 1)]
     sub_to = [sub] + [(chip + x) % chips * 2 + (core + c) % 2 for x, c in steps]

time: 47.9 us -> 50.5 us (1.054)
  Pallas kernels: 47 us -> 49.7 us
    pallas_call x1, Pallas kernels: 42.4 us -> 45.1 us  [fast(): pl.pallas_call(functools.partial(factors_kernel, n_dp, n_sub), out_shape=...]
where the time goes in v4:
time: 50.5 us; the launch traced here: 50.4 us
  Pallas kernels  49.7 us (98%)
  between operations  0.64 us (1%)
    pallas_call x1, Pallas kernels, fast(): pl.pallas_call(functools.partial(factors_kernel, n_dp, n_sub), out_shape=...  45.1 us
    pallas_call x1, Pallas kernels, fast(): pl.pallas_call(result_kernel, out_shape=(jax.ShapeDtypeStruct((block, cha...  4.63 us

profile of v4, /device:TPU:0, one launch (start us, length us, event | category | flops | bytes accessed | tf_op | source)
XLA Modules:
  0.0 50.4 jit_solution(1490097789074370208)
XLA Ops:
  0.6 45.1 %factors.1 = (bf16[96,1408]{1,0:T(8,128)(2,1)}, f32[32,1536]{1,0:T(8,128)}) custom-call(bf16[192,5632]{1,0:T(8,128)(2,1)} %a_hbm.1, bf16[192,1408]{1,0:T(8,128)(2,1)} %g_hbm.1, bf16[32,1408]{1,0:T(8,128)(2,1)} %bitcast.2), custom_call_target="tpu_custom_call" | custom-call | tf_op jit(solution)/shard_map/factors/pallas_call | solution.py:248
  45.7 4.6 %result.1 = (f32[1408,1408]{1,0:T(8,128)}, f32[32,1408]{1,0:T(8,128)}) custom-call(bf16[96,1408]{1,0:T(8,128)(2,1)} %get-tuple-element.6.left_hbm, f32[32,1536]{1,0:T(8,128)} %get-tuple-element.7.q_hbm), custom_call_target="tpu_custom_call" | custom-call | tf_op jit(solution)/shard_map/result/pallas_call | solution.py:289
